TPU v7x, 32 devices: a whole 2x2x4 slice. The times are simulated.
32 devices in a mesh: section: 8 (over z, y), expert: 4 (over x, core).
Axes of the slice: x: 2, y: 2, z: 4, core: 2. Of those that a mesh axis runs over, the one named last changes fastest.
Arguments:
- tokens: bfloat16 [8, 512, 3584], P('section', 'expert'), may hold values from -6 to 6
- norm_gain: float32 [8, 3584], P('section'), may hold values from 0.1 to 1.9
- expert_ids: int32 [8, 512, 2], P('section', 'expert'), may hold values from 0 to 3, all different within a row; in each aligned block of 128 rows (0 to 127, 128 to 255, ..., all dimensions but the last counted through in order) at most 80 rows name the same one
- gate_values: float32 [8, 512, 2], P('section', 'expert'), may hold values from 0.2 to 1
- gate_weight: bfloat16 [8, 3584, 8192], P('section', None, 'expert'), may hold values from -0.09375 to 0.09375
- up_weight: bfloat16 [8, 3584, 8192], P('section', None, 'expert'), may hold values from -0.09375 to 0.09375
- down_weight: bfloat16 [8, 8192, 3584], P('section', 'expert'), may hold values from -0.125 to 0.125
Outputs:
- handed: bfloat16 [8, 512, 3584], P('section', 'expert')
Inputs may be any that keep to these rules, and one draw needn't show every extreme that they name: `expert_ids`: each token names 2 different experts. Of the 128 tokens of one device (aligned blocks of 128 rows), at most 80 choose any one expert, and exactly 80 choose some expert in some blocks.
All inputs are finite; a program needn't handle non-finite values.
Results may differ from a plain program's by a relative error of at most 0.0053.
Values may be sent and summed in bfloat16 or wider, within the bound.
A program may use at most 128 MiB of HBM per device.

v0:
```python
import jax
import jax.numpy as jnp
from jax import lax
from jax.sharding import PartitionSpec as P

EXPERTS = 4
TOP = 2
CAP = 80


def shifted(shard, axis, by):
    devices = lax.axis_size(axis)
    return lax.ppermute(shard, axis, [(i, (i + by) % devices) for i in range(devices)])


def on_device(tokens, norm_gain, expert_ids, gate_values, gate_weight, up_weight, down_weight):
    resident = tokens[0]
    choice_ids = expert_ids[0]
    weights_in = gate_values[0]
    gate_local = gate_weight[0]
    up_local = up_weight[0]
    down_local = down_weight[0]
    owners = lax.axis_size("expert")
    shards = owners // EXPERTS
    tok_count = resident.shape[0]
    model_dim = resident.shape[1]
    capacity = CAP
    widened = resident.astype(jnp.float32)
    scale = lax.rsqrt(jnp.mean(widened * widened, axis=-1, keepdims=True) + 1e-06)
    normed = (widened * scale * norm_gain[0][None, :]).astype(jnp.bfloat16)
    flat_ids = choice_ids.reshape(-1)
    onehot = (flat_ids[:, None] == jnp.arange(EXPERTS, dtype=jnp.int32)[None, :]).astype(jnp.int32)
    position = jnp.cumsum(onehot, axis=0) - 1
    slot_of = jnp.sum(position * onehot, axis=1).reshape(tok_count, TOP)
    target = choice_ids * capacity + slot_of
    dispatch_matrix = jnp.sum(
        (
            target[:, :, None] == jnp.arange(EXPERTS * capacity, dtype=jnp.int32)[None, None, :]
        ).astype(jnp.bfloat16),
        axis=1,
    )
    outgoing = jnp.einsum(
        "tr,td->rd", dispatch_matrix, normed, preferred_element_type=jnp.float32
    ).astype(jnp.bfloat16)
    outgoing = jnp.repeat(outgoing.reshape(EXPERTS, capacity, model_dim), shards, axis=0)
    arrived = lax.all_to_all(outgoing, "expert", split_axis=0, concat_axis=0, tiled=True)
    sources = arrived.shape[0]
    count = arrived.shape[1]
    flat_rows = arrived.reshape(sources * count, model_dim)
    gate = jnp.dot(flat_rows, gate_local, preferred_element_type=jnp.float32)
    upward = jnp.dot(flat_rows, up_local, preferred_element_type=jnp.float32)
    hidden = (jax.nn.silu(gate) * upward).astype(jnp.bfloat16)
    partial_out = jnp.dot(hidden, down_local, preferred_element_type=jnp.float32).astype(
        jnp.bfloat16
    )
    partials = partial_out.reshape(sources, count, model_dim)
    returned = lax.all_to_all(partials, "expert", split_axis=0, concat_axis=0, tiled=True)
    summed = jnp.sum(
        returned.astype(jnp.float32).reshape(EXPERTS, shards, capacity, model_dim), axis=1
    )
    picked = summed.reshape(EXPERTS * capacity, model_dim)[target]
    mixture = jnp.sum(weights_in[:, :, None] * picked, axis=1)
    layer_out = (widened + mixture).astype(jnp.bfloat16)
    handed = shifted(layer_out, "section", 1)
    return handed[None]


def solution(mesh):
    in_specs = (
        P("section", "expert", None),
        P("section", None),
        P("section", "expert", None),
        P("section", "expert", None),
        P("section", None, "expert"),
        P("section", None, "expert"),
        P("section", "expert", None),
    )
    out_specs = P("section", "expert", None)
    return jax.shard_map(
        on_device, mesh=mesh, in_specs=in_specs, out_specs=out_specs, check_vma=False
    )
```

profile of v0, /device:TPU:1, one launch (start us, length us, event | category | flops | bytes accessed | tf_op | source)
XLA Modules:
  0.0 143.5 jit_solution(9372841574812305790)
XLA Ops:
  0.0 0.8 copy.19
  0.8 0.1 eq.42
  0.9 0.1 eq.38
  1.1 1.2 reduce-window.6
  2.3 0.1 slice.10
  2.4 0.1 copy.22
  2.5 0.1 copy.23
  2.6 0.1 add_bitcast_fusion
  2.7 0.1 reshape.91
  2.9 0.1 copy.24
  2.9 0.1 fusion.24
  3.0 1.4 %fusion.15 = f32[128]{0:T(128)S(1)} fusion(bf16[1,128,3584]{2,1,0:T(8,128)(2,1)} %param.7), kind=kLoop, calls=%fused_computation.16 | loop fusion | flops 1376128 | bytes 918016 | tf_op jit(solution)/shard_map/reduce_sum | solution.py:29
  4.5 0.8 reduce.1
  5.2 2.0 %convolution_convert_fusion = bf16[320,3584]{1,0:T(8,128)(2,1)S(1)} fusion(bf16[128,320]{0,1:T(8,128)(2,1)S(1)} %fusion.24, bf16[1,128,3584]{2,1,0:T(8,128)(2,1)} %param.7, f32[3584]{0:T(1024)S(1)} %reduce.1, f32[128]{0:T(128)S(1)} %add_rsqrt_fusion), kind=kOutput, calls=%fused_computation.8 | convolution fusion | flops 296583168 | bytes 3308032 | tf_op jit(solution)/shard_map/tr,td->rd/dot_general | solution.py:42
  7.3 0.0 slice-start
  7.3 31.4 %all_to_all.10 = bf16[4,80,3584]{2,1,0:T(8,128)(2,1)S(1)} all-to-all(bf16[4,80,3584]{2,1,0:T(8,128)(2,1)S(1)} %bitcast.58), channel_id=1, replica_groups=mesh['section'=8,'expert'=4] {'expert'}, dimensions={0} | all-to-all | bytes 4587520 | tf_op jit(solution)/shard_map/all_to_all | solution.py:46
  38.7 8.6 %fusion.4 = f32[320,2048]{1,0:T(8,128)S(1)} fusion(bf16[320,3584]{1,0:T(8,128)(2,1)S(1)} %bitcast.60, bf16[1,3584,2048]{2,1,0:T(8,128)(2,1)} %param.11), kind=kOutput, calls=%fused_computation.5 | convolution fusion | flops 4697620480 | bytes 19595264 | tf_op jit(solution)/shard_map/dot_general | solution.py:50
  47.3 5.1 %fusion.12 = bf16[320,2048]{1,0:T(8,128)(2,1)S(1)} fusion(bf16[320,3584]{1,0:T(8,128)(2,1)S(1)} %bitcast.61, bf16[1,3584,2048]{2,1,0:T(8,128)(2,1)S(1)} %bitcast.66, f32[320,2048]{1,0:T(8,128)S(1)} %fusion.4), kind=kOutput, calls=%fused_computation.14 | convolution fusion | flops 4701552640 | bytes 20905984 | tf_op jit(solution)/shard_map/dot_general | solution.py:51
  52.5 11.4 %fusion.6 = bf16[320,3584]{1,0:T(8,128)(2,1)} fusion(bf16[320,2048]{1,0:T(8,128)(2,1)S(1)} %fusion.12, bf16[1,2048,3584]{2,1,0:T(8,128)(2,1)} %param.13), kind=kOutput, calls=%fused_computation.7 | convolution fusion | flops 4698767360 | bytes 18284544 | tf_op jit(solution)/shard_map/dot_general | solution.py:53
  63.9 4.5 %all-to-all-start.1 = ((bf16[4,80,3584]{2,1,0:T(8,128)(2,1)}), bf16[4,80,3584]{2,1,0:T(8,128)(2,1)S(1)}, u32[]{:S(2)}, u32[]{:S(2)}) async-start(bf16[4,80,3584]{2,1,0:T(8,128)(2,1)} %bitcast.59), calls=%async_computation.1 | async-start | bytes 4587520 | tf_op jit(solution)/shard_map/all_to_all | solution.py:57
  68.4 0.1 reshape.96
  68.5 0.1 reshape.102
  68.7 0.1 copy.18
  68.8 26.5 %all-to-all-done.1 = bf16[4,80,3584]{2,1,0:T(8,128)(2,1)S(1)} async-done(((bf16[4,80,3584]{2,1,0:T(8,128)(2,1)}), bf16[4,80,3584]{2,1,0:T(8,128)(2,1)S(1)}, u32[]{:S(2)}, u32[]{:S(2)}) %all-to-all-start.1) | async-done | bytes 2293792 | tf_op jit(solution)/shard_map/all_to_all | solution.py:57
  95.3 2.8 %bitcast_convert_fusion = f32[320,3584]{1,0:T(8,128)} fusion(bf16[4,80,3584]{2,1,0:T(8,128)(2,1)S(1)} %all-to-all-done.1), kind=kLoop, calls=%fused_computation.15 | loop fusion | flops 1146880 | bytes 6881280 | tf_op jit(solution)/shard_map/reshape | solution.py:61
  98.0 7.5 %gather_fusion = f32[256,3584]{1,0:T(8,128)} fusion(f32[320,3584]{1,0:T(8,128)} %bitcast_convert_fusion, s32[1024]{0:T(1024)S(1)} %pad_clamp_fusion), kind=kCustom, calls=%fused_computation | custom fusion | bytes 7341056 | tf_op jit(solution)/shard_map/gather | solution.py:61
  105.5 5.5 %reshape.101 = f32[128,2,3584]{2,1,0:T(2,128)} reshape(f32[256,3584]{1,0:T(8,128)} %gather_fusion) | data formatting | bytes 7340032 | tf_op jit(solution)/shard_map/gather | solution.py:61
  111.0 7.4 %multiply_reduce_fusion = f32[128,3584]{1,0:T(8,128)S(1)} fusion(f32[128,2,3584]{2,1,0:T(2,128)} %reshape.101, f32[128,2]{1,0:T(8,128)S(1)} %copy.18), kind=kLoop, calls=%fused_computation.9 | loop fusion | flops 1376256 | bytes 5506048 | tf_op jit(solution)/shard_map/reduce_sum | solution.py:62
  118.4 0.2 fusion.18
  118.6 1.3 collective-permute-start
  119.9 22.7 %collective-permute-done = bf16[128,3584]{1,0:T(8,128)(2,1)S(1)} collective-permute-done((bf16[128,3584]{1,0:T(8,128)(2,1)S(1)}, bf16[128,3584]{1,0:T(8,128)(2,1)S(1)}, u32[]{:S(2)}, u32[]{:S(2)}) %collective-permute-start) | collective-permute-done | bytes 917536 | tf_op jit(solution)/shard_map/ppermute | solution.py:13
  142.6 0.9 copy.28
  (20 shorter events, 0.1 us)
Async XLA Ops:
  7.3 40.0 %slice-start = ((s8[14680064]{0:T(1024)(128)(4,1)}), s8[4194304]{0:T(1024)(128)(4,1)S(1)}, s32[]{:S(2)}) async-start(s8[14680064]{0:T(1024)(128)(4,1)} %bitcast.65), calls=%async_computation.2 | async-start | bytes 8388608
  38.7 8.6 %slice-start.1 = ((s8[14680064]{0:T(1024)(128)(4,1)}), s8[4194304]{0:T(1024)(128)(4,1)S(1)}, s32[]{:S(2)}) async-start(s8[14680064]{0:T(1024)(128)(4,1)} %bitcast.65), calls=%async_computation.3 | async-start | bytes 8388608
  38.7 8.6 %slice-start.2 = ((s8[14680064]{0:T(1024)(128)(4,1)}), s8[4194304]{0:T(1024)(128)(4,1)S(1)}, s32[]{:S(2)}) async-start(s8[14680064]{0:T(1024)(128)(4,1)} %bitcast.65), calls=%async_computation.4 | async-start | bytes 8388608
  38.7 8.6 %slice-start.3 = ((s8[14680064]{0:T(1024)(128)(4,1)}), s8[2097152]{0:T(1024)(128)(4,1)S(1)}, s32[]{:S(2)}) async-start(s8[14680064]{0:T(1024)(128)(4,1)} %bitcast.65), calls=%async_computation.5 | async-start | bytes 4194304
  63.9 4.8 %copy-start.1 = (f32[1,128,2]{1,2,0:T(2,128)S(1)}, f32[1,128,2]{1,2,0:T(2,128)}, u32[]{:S(2)}) copy-start(f32[1,128,2]{1,2,0:T(2,128)} %param.10) | copy-start | bytes 3076
  63.9 31.4 %all-to-all-start.1 = ((bf16[4,80,3584]{2,1,0:T(8,128)(2,1)}), bf16[4,80,3584]{2,1,0:T(8,128)(2,1)S(1)}, u32[]{:S(2)}, u32[]{:S(2)}) async-start(bf16[4,80,3584]{2,1,0:T(8,128)(2,1)} %bitcast.59), calls=%async_computation.1 | async-start | bytes 4587520 | tf_op jit(solution)/shard_map/all_to_all | solution.py:57
  111.0 7.4 %copy-start = (bf16[1,128,3584]{2,1,0:T(8,128)(2,1)S(1)}, bf16[1,128,3584]{2,1,0:T(8,128)(2,1)}, u32[]{:S(2)}) copy-start(bf16[1,128,3584]{2,1,0:T(8,128)(2,1)} %param.7) | copy-start | bytes 2752516
  118.6 24.0 %collective-permute-start = (bf16[128,3584]{1,0:T(8,128)(2,1)S(1)}, bf16[128,3584]{1,0:T(8,128)(2,1)S(1)}, u32[]{:S(2)}, u32[]{:S(2)}) collective-permute-start(bf16[128,3584]{1,0:T(8,128)(2,1)S(1)} %fusion.18), channel_id=1, source_target_pairs={{0,4},{4,8},{8,12},{12,16},{16,20},{20,24},{24,28},{28,0},{1,5},{5... | collective-permute-start | bytes 2752520 | tf_op jit(solution)/shard_map/ppermute | solution.py:13
where the time goes:
time: 146 us; the launch traced here: 144 us
  waiting for transfers between devices  49.2 us (34%)
  blocking collectives  31.4 us (22%)
  matrix products  27.2 us (19%)
  local copies, waits for them, and re-layouts  15.8 us (11%)
  other arithmetic  14 us (10%)
  starting transfers between devices  5.76 us (4%)
    all_to_all x1, blocking collectives, on_device(): lax.all_to_all(outgoing, 'expert', split_axis=0, concat_axis=0, tiled=True)  31.4 us
    all_to_all x1, waiting for transfers between devices, on_device(): lax.all_to_all(partials, 'expert', split_axis=0, concat_axis=0, tiled=True)  26.5 us
    ppermute x1, waiting for transfers between devices, shifted(): lax.ppermute(shard, axis, [(i, (i + by) % devices) for i in range(devices)])  22.7 us
    gather x2, local copies, waits for them, and re-layouts, on_device(): picked = summed.reshape(EXPERTS * capacity, model_dim)[target]  13 us
    dot_general x1, matrix products, on_device(): jnp.dot(hidden, down_local, preferred_element_type=jnp.float32)  11.4 us
    dot_general x1, matrix products, on_device(): gate = jnp.dot(flat_rows, gate_local, preferred_element_type=jnp.float32)  8.6 us
    reduce_sum x1, other arithmetic, on_device(): mixture = jnp.sum(weights_in[:, :, None] * picked, axis=1)  7.4 us
    dot_general x1, matrix products, on_device(): upward = jnp.dot(flat_rows, up_local, preferred_element_type=jnp.float32)  5.14 us
  transfers between devices with their start and end apart: 2, of which 2 were waited for; matrix products, arithmetic and copies ran while one was open for 0% of the time, Pallas kernels for 0%

commit v1 on v0

--- a/solution.py
+++ b/solution.py
@@ -1,11 +1,374 @@
+import functools
+
 import jax
 import jax.numpy as jnp
 from jax import lax
+from jax.experimental import pallas as pl
+from jax.experimental.pallas import tpu as pltpu
 from jax.sharding import PartitionSpec as P
 
 EXPERTS = 4
 TOP = 2
 CAP = 80
+MESH = pl.DeviceIdType.MESH
+F32 = jnp.float32
+BF16 = jnp.bfloat16
+UP_CHUNKS = 4
+WIDE = 512
+NARROW = 256
+STEP = 16
+
+
+def kernel(
+    sections, tok, gain, ids, gates, gate_hbm, up_hbm, down_hbm, out,
+    gate_w, up_w, down_w, nrm, meta, pick, scale, rows_in, hidden, base, local_out, local_in,
+    far_out, far_in, back,
+    w_sem, meta_s, meta_r, sib_s, sib_r, x_s, x_r, relay_s, relay_r, local_s, local_r,
+    swap_s, swap_r, back_s, back_r, hand_s, hand_r,
+):
+    tokens, model = tok.shape
+    units = gate_w.shape[1]
+    half = tokens // 2
+    steps = half // STEP
+    section = lax.axis_index("section")
+    me = lax.axis_index("expert")
+    chip = lax.div(me, 2)
+    core = lax.rem(me, 2)
+    other = 1 - core
+    sibling = chip * 2 + other
+    far_chip = (1 - chip) * 2
+    after = lax.rem(section + 1, sections)
+    before = lax.rem(section + sections - 1, sections)
+    mine = pl.ds(pl.multiple_of(core * half, half), half)
+    theirs = pl.ds(pl.multiple_of(other * half, half), half)
+
+    def remote(src, dst, send, recv, **device):
+        return pltpu.make_async_remote_copy(
+            src_ref=src, dst_ref=dst, send_sem=send, recv_sem=recv,
+            device_id=device, device_id_type=MESH,
+        )
+
+    barrier = pltpu.get_barrier_semaphore()
+    for peer in (sibling, far_chip, far_chip + 1):
+        pl.semaphore_signal(barrier, inc=1, device_id={"expert": peer}, device_id_type=MESH)
+    for peer in (after, before):
+        pl.semaphore_signal(barrier, inc=1, device_id={"section": peer}, device_id_type=MESH)
+
+    up_width = units // UP_CHUNKS
+
+    def gate_copy(k):
+        cols = pl.ds(pl.multiple_of(k * up_width, up_width), up_width)
+        return pltpu.make_async_copy(gate_hbm.at[:, cols], gate_w.at[:, cols], w_sem.at[k])
+
+    def up_copy(k):
+        cols = pl.ds(pl.multiple_of(k * up_width, up_width), up_width)
+        return pltpu.make_async_copy(up_hbm.at[:, cols], up_w.at[:, cols], w_sem.at[UP_CHUNKS + k])
+
+    def down_copy(k):
+        cols = pl.ds(pl.multiple_of(k * WIDE, WIDE), WIDE)
+        return pltpu.make_async_copy(
+            down_hbm.at[:, cols], down_w.at[:, cols], w_sem.at[2 * UP_CHUNKS + k]
+        )
+
+    for k in range(UP_CHUNKS):
+        gate_copy(k).start()
+        up_copy(k).start()
+    for k in range(model // WIDE):
+        down_copy(k).start()
+
+    meta[0] = jnp.zeros(meta.shape[1:], F32)
+    meta[0, 0:TOP, :] = ids[...].astype(F32)
+    meta[0, TOP:2 * TOP, :] = gates[...]
+
+    @pl.loop(0, tokens // STEP)
+    def _(i):
+        rows = pl.ds(pl.multiple_of(i * STEP, STEP), STEP)
+        widened = tok[rows, :].astype(F32)
+        inverse = lax.rsqrt(jnp.mean(widened * widened, axis=-1, keepdims=True) + 1e-06)
+        nrm[0, rows, :] = (widened * inverse * gain[...]).astype(BF16)
+
+    pl.semaphore_wait(barrier, 5)
+
+    def sib_copy(k, rows):
+        return remote(
+            nrm.at[0, rows], nrm.at[1, rows], sib_s.at[k], sib_r.at[k], expert=sibling
+        )
+
+    def x_copy(source):
+        slot = lax.rem(source + 2 - core, 2)
+        return remote(
+            nrm.at[slot, mine], nrm.at[2 + source, mine], x_s.at[source], x_r.at[source],
+            expert=far_chip + core,
+        )
+
+    def relay_copy(source, rows):
+        return remote(
+            nrm.at[2 + source, rows], nrm.at[2 + source, rows], relay_s.at[source],
+            relay_r.at[source], expert=sibling,
+        )
+
+    meta_copies = [
+        remote(meta.at[0], meta.at[1], meta_s.at[0], meta_r.at[0], expert=sibling),
+        remote(meta.at[0], meta.at[2 + core], meta_s.at[1], meta_r.at[1 + core], expert=far_chip),
+        remote(
+            meta.at[0], meta.at[2 + core], meta_s.at[2], meta_r.at[1 + core], expert=far_chip + 1
+        ),
+    ]
+    sib_copy(0, theirs).start()
+
+    @pl.when(core == 0)
+    def _():
+        x_copy(0).start()
+
+    for copy in meta_copies:
+        copy.start()
+    sib_copy(1, mine).start()
+    sib_copy(0, mine).wait_recv()
+
+    @pl.when(core == 1)
+    def _():
+        x_copy(0).start()
+
+    x_copy(1).start()
+
+    def meta_arrived(slot):
+        remote(
+            meta.at[0], meta.at[slot], meta_s.at[0], meta_r.at[slot - 1], expert=sibling
+        ).wait_recv()
+
+    def gather(slot, place):
+        expert = me.astype(F32)
+        about = meta[slot]
+        first = about[0:1, :] == expert
+        second = about[1:2, :] == expert
+        chosen = jnp.where(first, 1.0, 0.0) + jnp.where(second, 1.0, 0.0)
+        weight = jnp.where(first, about[2:3, :], 0.0) + jnp.where(second, about[3:4, :], 0.0)
+        upper = jnp.where(
+            lax.broadcasted_iota(jnp.int32, (tokens, tokens), 0)
+            < lax.broadcasted_iota(jnp.int32, (tokens, tokens), 1),
+            1.0, 0.0,
+        ).astype(BF16)
+        ahead = jnp.dot(
+            jnp.broadcast_to(chosen, (16, tokens)).astype(BF16), upper,
+            preferred_element_type=F32,
+        )[0:1, :]
+        wanted = lax.broadcasted_iota(jnp.int32, (CAP, tokens), 0).astype(F32)
+        picked = jnp.where(ahead == wanted, 1.0, 0.0) * chosen
+        pick[place] = picked.astype(BF16)
+        scale[place] = jnp.broadcast_to(
+            jnp.sum(picked * weight, axis=1, keepdims=True), (CAP, scale.shape[2])
+        )
+
+        @pl.loop(0, model // WIDE)
+        def _(n):
+            cols = pl.ds(pl.multiple_of(n * WIDE, WIDE), WIDE)
+            rows_in[place * CAP:(place + 1) * CAP, cols] = jnp.dot(
+                pick[place], nrm[slot, :, cols], preferred_element_type=F32
+            ).astype(BF16)
+
+    def up_tile(count, i):
+        cols = pl.ds(pl.multiple_of(i * NARROW, NARROW), NARROW)
+        gate = jnp.dot(rows_in[0:count, :], gate_w[:, cols], preferred_element_type=F32)
+        upward = jnp.dot(rows_in[0:count, :], up_w[:, cols], preferred_element_type=F32)
+        hidden[0:count, cols] = (jax.nn.silu(gate) * upward).astype(BF16)
+
+    def spread(place, product):
+        weighted = (
+            product[place * CAP:(place + 1) * CAP, :] * scale[place][:, 0:1]
+        ).astype(BF16)
+        return lax.dot_general(
+            pick[place], weighted, (((0,), (0,)), ((), ())), preferred_element_type=F32
+        )
+
+    def swap_copy(source, rows):
+        return remote(
+            far_out.at[source, rows], far_in.at[source], swap_s.at[source], swap_r.at[source],
+            expert=sibling,
+        )
+
+    def back_copy(source, q):
+        rows = pl.ds(pl.multiple_of(core * half + q * STEP, STEP), STEP)
+        return remote(
+            far_out.at[source, rows], back.at[rows], back_s.at[source * steps + q],
+            back_r.at[core * steps + q], expert=far_chip + source,
+        )
+
+    def send_back(source):
+        swap_copy(source, theirs).wait_recv()
+
+        @pl.loop(0, steps)
+        def _(q):
+            rows = pl.ds(pl.multiple_of(core * half + q * STEP, STEP), STEP)
+            near = pl.ds(pl.multiple_of(q * STEP, STEP), STEP)
+            far_out[source, rows, :] = (
+                far_out[source, rows, :].astype(F32) + far_in[source, near, :].astype(F32)
+            ).astype(BF16)
+            back_copy(source, q).start()
+
+    def hand_copy(sender, q):
+        rows = pl.ds(pl.multiple_of(sender * half + q * STEP, STEP), STEP)
+        return remote(
+            back.at[rows], out.at[rows], hand_s.at[sender * steps + q],
+            hand_r.at[sender * steps + q], section=after,
+        )
+
+    def finish(q):
+        for sender in range(2):
+            rows = pl.ds(pl.multiple_of(sender * half + q * STEP, STEP), STEP)
+            remote(
+                back.at[rows], back.at[rows], back_s.at[0], back_r.at[sender * steps + q],
+                expert=far_chip,
+            ).wait_recv()
+            total = base[rows, :] + local_in[rows, :].astype(F32) + back[rows, :].astype(F32)
+            back[rows, :] = total.astype(BF16)
+            hand_copy(sender, q).start()
+
+    local_copy = remote(
+        local_out, local_in, local_s.at[0], local_r.at[0], expert=sibling
+    )
+
+    gather(0, 0)
+    sib_copy(1, theirs).wait_recv()
+    meta_arrived(1)
+    gather(1, 1)
+
+    @pl.loop(0, UP_CHUNKS)
+    def _(k):
+        gate_copy(k).wait()
+        up_copy(k).wait()
+
+        @pl.loop(0, up_width // NARROW)
+        def _(i):
+            up_tile(2 * CAP, k * (up_width // NARROW) + i)
+
+    @pl.loop(0, model // WIDE)
+    def _(n):
+        down_copy(n).wait()
+        cols = pl.ds(pl.multiple_of(n * WIDE, WIDE), WIDE)
+        product = jnp.dot(hidden[...], down_w[:, cols], preferred_element_type=F32)
+        base[:, cols] = tok[:, cols].astype(F32) + spread(0, product)
+        local_out[:, cols] = spread(1, product).astype(BF16)
+
+        @pl.when(n == 3)
+        def _():
+            x_copy(0).wait_recv()
+            relay_copy(0, mine).start()
+
+    local_copy.start()
+
+    for source in range(2):
+        if source == 1:
+            x_copy(1).wait_recv()
+            relay_copy(1, mine).start()
+            send_back(0)
+        relay_copy(source, theirs).wait_recv()
+        meta_arrived(2 + source)
+        gather(2 + source, 0)
+
+        @pl.loop(0, units // NARROW)
+        def _(i):
+            up_tile(CAP, i)
+
+        if source == 1:
+            local_copy.wait_recv()
+
+        @pl.loop(0, model // WIDE)
+        def _(n):
+            cols = pl.ds(pl.multiple_of(n * WIDE, WIDE), WIDE)
+            product = jnp.dot(hidden[0:CAP, :], down_w[:, cols], preferred_element_type=F32)
+            far_out[source, :, cols] = spread(0, product).astype(BF16)
+            if source == 1:
+                @pl.when((core == 0) & ((n == 0) | (n == 4)))
+                def _():
+                    finish(lax.div(n, 4))
+
+        swap_copy(source, theirs).start()
+
+    send_back(1)
+
+    @pl.when(core == 0)
+    def _():
+        @pl.loop(2, steps)
+        def _(q):
+            finish(q)
+
+    @pl.when(core == 1)
+    def _():
+        @pl.loop(0, steps)
+        def _(q):
+            finish(q)
+
+    for sender in range(2):
+        for q in range(steps):
+            hand_copy(sender, q).wait()
+    for source in range(2):
+        for q in range(steps):
+            back_copy(source, q).wait_send()
+        swap_copy(source, theirs).wait_send()
+        x_copy(source).wait_send()
+        relay_copy(source, mine).wait_send()
+    sib_copy(0, theirs).wait_send()
+    sib_copy(1, mine).wait_send()
+    for copy in meta_copies:
+        copy.wait_send()
+    local_copy.wait_send()
+
+
+def two_chips(sections, tokens, norm_gain, expert_ids, gate_values, gate_weight, up_weight, down_weight):
+    count, model = tokens.shape[1:]
+    units = gate_weight.shape[2]
+    half = count // 2
+    steps = half // STEP
+    rows = 2 * CAP
+    dma = pltpu.SemaphoreType.DMA
+    vmem = pl.BlockSpec(memory_space=pltpu.VMEM)
+    hbm = pl.BlockSpec(memory_space=pl.ANY)
+    handed = pl.pallas_call(
+        functools.partial(kernel, sections),
+        out_shape=jax.ShapeDtypeStruct((count, model), BF16),
+        in_specs=[vmem, vmem, vmem, vmem, hbm, hbm, hbm],
+        out_specs=hbm,
+        scratch_shapes=[
+            pltpu.VMEM((model, units), BF16),
+            pltpu.VMEM((model, units), BF16),
+            pltpu.VMEM((units, model), BF16),
+            pltpu.VMEM((4, count, model), BF16),
+            pltpu.VMEM((4, 8, count), F32),
+            pltpu.VMEM((2, CAP, count), BF16),
+            pltpu.VMEM((2, CAP, 128), F32),
+            pltpu.VMEM((rows, model), BF16),
+            pltpu.VMEM((rows, units), BF16),
+            pltpu.VMEM((count, model), F32),
+            pltpu.VMEM((count, model), BF16),
+            pltpu.VMEM((count, model), BF16),
+            pltpu.VMEM((2, count, model), BF16),
+            pltpu.VMEM((2, half, model), BF16),
+            pltpu.VMEM((count, model), BF16),
+            dma((2 * UP_CHUNKS + model // WIDE,)),
+            dma((3,)), dma((3,)),
+            dma((2,)), dma((2,)),
+            dma((2,)), dma((2,)),
+            dma((2,)), dma((2,)),
+            dma((1,)), dma((1,)),
+            dma((2,)), dma((2,)),
+            dma((2 * steps,)), dma((2 * steps,)),
+            dma((2 * steps,)), dma((2 * steps,)),
+        ],
+        compiler_params=pltpu.CompilerParams(
+            collective_id=0, has_side_effects=True, vmem_limit_bytes=VMEM_LIMIT
+        ),
+        cost_estimate=pl.CostEstimate(
+            flops=6 * EXPERTS * CAP * model * units, bytes_accessed=6 * model * units,
+            transcendentals=EXPERTS * CAP * units,
+        ),
+    )(
+        tokens[0], norm_gain, expert_ids[0].T, gate_values[0].T,
+        gate_weight[0], up_weight[0], down_weight[0],
+    )
+    return handed[None]
+
+
+VMEM_LIMIT = 63 * 1024 * 1024
 
 
 def shifted(shard, axis, by):
@@ -76,6 +439,10 @@
         P("section", "expert", None),
     )
     out_specs = P("section", "expert", None)
+    if mesh.shape["expert"] == EXPERTS:
+        on_one = functools.partial(two_chips, mesh.shape["section"])
+    else:
+        on_one = on_device
     return jax.shard_map(
-        on_device, mesh=mesh, in_specs=in_specs, out_specs=out_specs, check_vma=False
-    )
+        on_one, mesh=mesh, in_specs=in_specs, out_specs=out_specs, check_vma=False
+    )

time: 146 us -> 71.7 us (0.49); the launches traced: 144 us -> 71.5 us
  Pallas kernels: 0 us -> 69.3 us
  waiting for transfers between devices: 49.2 us -> 0 us
  blocking collectives: 31.4 us -> 0 us
  matrix products: 27.2 us -> 0 us
  other arithmetic: 14 us -> 0 us
  local copies, waits for them, and re-layouts: 15.8 us -> 2.16 us
  starting transfers between devices: 5.76 us -> 0 us
    pallas_call x0 -> x1, Pallas kernels: none -> 69.3 us  [two_chips(): pl.pallas_call(functools.partial(kernel, sections), out_shape=jax.ShapeDt...]
    all_to_all x1 -> x0, blocking collectives: 31.4 us -> none  [on_device(): lax.all_to_all(outgoing, 'expert', split_axis=0, concat_axis=0, tiled=True)]
    dot_general x4 -> x0, matrix products: 27.2 us -> none  [the longest x1 11.4 us: on_device(): jnp.dot(hidden, down_local, preferred_element_type=jnp.float32)]
    all_to_all x1 -> x0, waiting for transfers between devices: 26.5 us -> none  [on_device(): lax.all_to_all(partials, 'expert', split_axis=0, concat_axis=0, tiled=True)]
    ppermute x1 -> x0, waiting for transfers between devices: 22.7 us -> none  [shifted(): lax.ppermute(shard, axis, [(i, (i + by) % devices) for i in range(devices)])]
    gather x2 -> x0, local copies, waits for them, and re-layouts: 13 us -> none  [on_device(): picked = summed.reshape(EXPERTS * capacity, model_dim)[target]]
    reduce_sum x4 -> x0, other arithmetic: 8.93 us -> none  [the longest x1 7.4 us: on_device(): mixture = jnp.sum(weights_in[:, :, None] * picked, axis=1)]
    all_to_all x1 -> x0, starting transfers between devices: 4.48 us -> none  [on_device(): lax.all_to_all(partials, 'expert', split_axis=0, concat_axis=0, tiled=True)]
  transfers between devices with their start and end apart: 2 -> 0, of which waited for: 2 -> 0; matrix products, arithmetic and copies ran while one was open for 0% -> 0% of each run, Pallas kernels for 0% -> 0%
where the time goes in v1:
time: 71.7 us; the launch traced here: 71.5 us
  Pallas kernels  69.3 us (97%)
  local copies, waits for them, and re-layouts  2.16 us (3%)
    pallas_call x1, Pallas kernels, two_chips(): pl.pallas_call(functools.partial(kernel, sections), out_shape=jax.ShapeDt...  69.3 us
    unnamed x1, local copies, waits for them, and re-layouts  2.16 us

profile of v1, /device:TPU:1, one launch (start us, length us, event | category | flops | bytes accessed | tf_op | source)
XLA Modules:
  0.0 71.5 jit_solution(13441544942497732696)
XLA Ops:
  0.0 69.3 %shard_map.73 = bf16[128,3584]{1,0:T(8,128)(2,1)} custom-call(bf16[128,3584]{1,0:T(8,128)(2,1)} %bitcast.15, f32[1,3584]{1,0:T(1,128)} %gain.1, s32[2,128]{1,0:T(2,128)} %bitcast.16, f32[2,128]{1,0:T(2,128)} %bitcast.17, bf16[3584,2048]{1,0:T(8,128)(2,1)} %bitcast.12, bf16[3584,2048]{1,0:T(8,128)(2,1)} %bitcast.13, bf16[2048,3584]{1,0:T(8,128)(2,1)} %bitcast.14), custom_call_target="tpu_custom_call" | custom-call | flops 14092861440 | bytes 44040192 | tf_op jit(solution)/shard_map/pallas_call | solution.py:326
  69.3 2.2 %copy.9 = bf16[1,128,3584]{2,1,0:T(8,128)(2,1)} copy(bf16[1,128,3584]{2,1,0:T(8,128)(2,1)} %bitcast.11) | data formatting | bytes 1835008

commit v2 on v1

--- a/solution.py
+++ b/solution.py
@@ -17,6 +17,7 @@
 WIDE = 512
 NARROW = 256
 STEP = 16
+COPIES = 8
 
 
 def kernel(
@@ -29,7 +30,7 @@
     tokens, model = tok.shape
     units = gate_w.shape[1]
     half = tokens // 2
-    steps = half // STEP
+    tiles = model // WIDE
     section = lax.axis_index("section")
     me = lax.axis_index("expert")
     chip = lax.div(me, 2)
@@ -180,57 +181,91 @@
             pick[place], weighted, (((0,), (0,)), ((), ())), preferred_element_type=F32
         )
 
-    def swap_copy(source, rows):
-        return remote(
-            far_out.at[source, rows], far_in.at[source], swap_s.at[source], swap_r.at[source],
+    def wide(n):
+        return pl.ds(pl.multiple_of(n * WIDE, WIDE), WIDE)
+
+    def local_copy(n):
+        return remote(
+            local_out.at[:, wide(n)], local_in.at[:, wide(n)], local_s.at[n], local_r.at[n],
             expert=sibling,
         )
 
-    def back_copy(source, q):
-        rows = pl.ds(pl.multiple_of(core * half + q * STEP, STEP), STEP)
-        return remote(
-            far_out.at[source, rows], back.at[rows], back_s.at[source * steps + q],
-            back_r.at[core * steps + q], expert=far_chip + source,
-        )
-
-    def send_back(source):
-        swap_copy(source, theirs).wait_recv()
-
-        @pl.loop(0, steps)
-        def _(q):
-            rows = pl.ds(pl.multiple_of(core * half + q * STEP, STEP), STEP)
-            near = pl.ds(pl.multiple_of(q * STEP, STEP), STEP)
-            far_out[source, rows, :] = (
-                far_out[source, rows, :].astype(F32) + far_in[source, near, :].astype(F32)
+    def swap_copy(source, n):
+        return remote(
+            far_out.at[source, theirs, wide(n)], far_in.at[source, :, wide(n)],
+            swap_s.at[source * tiles + n], swap_r.at[source * tiles + n], expert=sibling,
+        )
+
+    def back_copy(source, n):
+        return remote(
+            far_out.at[source, mine, wide(n)], back.at[mine, wide(n)],
+            back_s.at[source * tiles + n], back_r.at[core * tiles + n],
+            expert=far_chip + source,
+        )
+
+    def hand_copy(n):
+        return remote(
+            back.at[:, wide(n)], out.at[:, wide(n)], hand_s.at[n], hand_r.at[n], section=after
+        )
+
+    def settle(source, n):
+        swap_copy(source, n).wait_recv()
+        far_out[source, mine, wide(n)] = (
+            far_out[source, mine, wide(n)].astype(F32) + far_in[source, :, wide(n)].astype(F32)
+        ).astype(BF16)
+        back_copy(source, n).start()
+
+    def finish(n):
+        local_copy(n).wait_recv()
+        for sender in range(2):
+            rows = pl.ds(sender * half, half)
+            remote(
+                back.at[rows, wide(n)], back.at[rows, wide(n)], back_s.at[0],
+                back_r.at[sender * tiles + n], expert=far_chip,
+            ).wait_recv()
+        for first in range(0, tokens, 32):
+            rows = pl.ds(first, 32)
+            back[rows, wide(n)] = (
+                base[rows, wide(n)] + local_in[rows, wide(n)].astype(F32)
+                + back[rows, wide(n)].astype(F32)
             ).astype(BF16)
-            back_copy(source, q).start()
-
-    def hand_copy(sender, q):
-        rows = pl.ds(pl.multiple_of(sender * half + q * STEP, STEP), STEP)
-        return remote(
-            back.at[rows], out.at[rows], hand_s.at[sender * steps + q],
-            hand_r.at[sender * steps + q], section=after,
-        )
-
-    def finish(q):
-        for sender in range(2):
-            rows = pl.ds(pl.multiple_of(sender * half + q * STEP, STEP), STEP)
-            remote(
-                back.at[rows], back.at[rows], back_s.at[0], back_r.at[sender * steps + q],
-                expert=far_chip,
-            ).wait_recv()
-            total = base[rows, :] + local_in[rows, :].astype(F32) + back[rows, :].astype(F32)
-            back[rows, :] = total.astype(BF16)
-            hand_copy(sender, q).start()
-
-    local_copy = remote(
-        local_out, local_in, local_s.at[0], local_r.at[0], expert=sibling
-    )
+        hand_copy(n).start()
+
+    def down_pass(source, place, extra):
+        @pl.loop(0, tiles)
+        def _(n):
+            if source == 0:
+                down_copy(n).wait()
+            for part in range(WIDE // NARROW):
+                cols = pl.ds(pl.multiple_of(n * WIDE + part * NARROW, NARROW), NARROW)
+                product = jnp.dot(
+                    hidden[0:(place + 1) * CAP, :], down_w[:, cols], preferred_element_type=F32
+                )
+                far_out[source, :, cols] = spread(place, product).astype(BF16)
+                if source == 0:
+                    base[:, cols] = tok[:, cols].astype(F32) + spread(0, product)
+                    local_out[:, cols] = spread(1, product).astype(BF16)
+            swap_copy(source, n).start()
+            if source == 0:
+                local_copy(n).start()
+
+            @pl.when(n > 0)
+            def _():
+                settle(source, n - 1)
+
+            extra(n)
+
+        settle(source, tiles - 1)
 
     gather(0, 0)
     sib_copy(1, theirs).wait_recv()
     meta_arrived(1)
     gather(1, 1)
+    x_copy(0).wait_recv()
+    relay_copy(0, mine).start()
+    meta_arrived(2)
+    relay_copy(0, theirs).wait_recv()
+    gather(2, 2)
 
     @pl.loop(0, UP_CHUNKS)
     def _(k):
@@ -239,87 +274,85 @@
 
         @pl.loop(0, up_width // NARROW)
         def _(i):
-            up_tile(2 * CAP, k * (up_width // NARROW) + i)
-
-    @pl.loop(0, model // WIDE)
-    def _(n):
-        down_copy(n).wait()
-        cols = pl.ds(pl.multiple_of(n * WIDE, WIDE), WIDE)
-        product = jnp.dot(hidden[...], down_w[:, cols], preferred_element_type=F32)
-        base[:, cols] = tok[:, cols].astype(F32) + spread(0, product)
-        local_out[:, cols] = spread(1, product).astype(BF16)
-
-        @pl.when(n == 3)
+            up_tile(3 * CAP, k * (up_width // NARROW) + i)
+
+    def relay_next(n):
+        @pl.when(n == tiles - 2)
         def _():
-            x_copy(0).wait_recv()
-            relay_copy(0, mine).start()
-
-    local_copy.start()
-
-    for source in range(2):
-        if source == 1:
             x_copy(1).wait_recv()
             relay_copy(1, mine).start()
-            send_back(0)
-        relay_copy(source, theirs).wait_recv()
-        meta_arrived(2 + source)
-        gather(2 + source, 0)
-
-        @pl.loop(0, units // NARROW)
-        def _(i):
-            up_tile(CAP, i)
-
-        if source == 1:
-            local_copy.wait_recv()
-
-        @pl.loop(0, model // WIDE)
-        def _(n):
-            cols = pl.ds(pl.multiple_of(n * WIDE, WIDE), WIDE)
-            product = jnp.dot(hidden[0:CAP, :], down_w[:, cols], preferred_element_type=F32)
-            far_out[source, :, cols] = spread(0, product).astype(BF16)
-            if source == 1:
-                @pl.when((core == 0) & ((n == 0) | (n == 4)))
-                def _():
-                    finish(lax.div(n, 4))
-
-        swap_copy(source, theirs).start()
-
-    send_back(1)
+
+    down_pass(0, 2, relay_next)
+
+    meta_arrived(3)
+    relay_copy(1, theirs).wait_recv()
+    gather(3, 0)
+    early = units // NARROW // 2 - 1
+
+    @pl.loop(0, units // NARROW)
+    def _(i):
+        up_tile(CAP, i)
+
+        @pl.when((core == 0) & (i >= 2) & (lax.rem(i, 2) == 0))
+        def _():
+            finish(lax.div(i, 2) - 1)
+
+    def hand_early(n):
+        @pl.when((core == 0) & (n < 5) & (lax.rem(n, 2) == 0))
+        def _():
+            finish(early + lax.div(n, 2))
+
+    down_pass(1, 0, hand_early)
 
     @pl.when(core == 0)
     def _():
-        @pl.loop(2, steps)
-        def _(q):
-            finish(q)
+        @pl.loop(early + 3, tiles)
+        def _(n):
+            finish(n)
 
     @pl.when(core == 1)
     def _():
-        @pl.loop(0, steps)
-        def _(q):
-            finish(q)
-
-    for sender in range(2):
-        for q in range(steps):
-            hand_copy(sender, q).wait()
+        @pl.loop(0, tiles)
+        def _(n):
+            finish(n)
+
+    @pl.loop(0, tiles)
+    def _(n):
+        hand_copy(n).wait()
+        local_copy(n).wait_send()
+        for source in range(2):
+            back_copy(source, n).wait_send()
+            swap_copy(source, n).wait_send()
+
     for source in range(2):
-        for q in range(steps):
-            back_copy(source, q).wait_send()
-        swap_copy(source, theirs).wait_send()
         x_copy(source).wait_send()
         relay_copy(source, mine).wait_send()
     sib_copy(0, theirs).wait_send()
     sib_copy(1, mine).wait_send()
     for copy in meta_copies:
         copy.wait_send()
-    local_copy.wait_send()
+
+
+def copy_out(src, dst, sem):
+    rows = src.shape[0] // COPIES
+    copies = [
+        pltpu.make_async_copy(
+            src.at[pl.ds(k * rows, rows)], dst.at[pl.ds(k * rows, rows)], sem.at[k]
+        )
+        for k in range(COPIES)
+    ]
+    for copy in copies:
+        copy.start()
+    for copy in copies:
+        copy.wait()
 
 
 def two_chips(sections, tokens, norm_gain, expert_ids, gate_values, gate_weight, up_weight, down_weight):
     count, model = tokens.shape[1:]
     units = gate_weight.shape[2]
     half = count // 2
-    steps = half // STEP
-    rows = 2 * CAP
+    tiles = model // WIDE
+    rows = 3 * CAP
     dma = pltpu.SemaphoreType.DMA
     vmem = pl.BlockSpec(memory_space=pltpu.VMEM)
     hbm = pl.BlockSpec(memory_space=pl.ANY)
@@ -334,8 +367,8 @@
             pltpu.VMEM((units, model), BF16),
             pltpu.VMEM((4, count, model), BF16),
             pltpu.VMEM((4, 8, count), F32),
-            pltpu.VMEM((2, CAP, count), BF16),
-            pltpu.VMEM((2, CAP, 128), F32),
+            pltpu.VMEM((3, CAP, count), BF16),
+            pltpu.VMEM((3, CAP, 128), F32),
             pltpu.VMEM((rows, model), BF16),
             pltpu.VMEM((rows, units), BF16),
             pltpu.VMEM((count, model), F32),
@@ -349,10 +382,10 @@
             dma((2,)), dma((2,)),
             dma((2,)), dma((2,)),
             dma((2,)), dma((2,)),
-            dma((1,)), dma((1,)),
-            dma((2,)), dma((2,)),
-            dma((2 * steps,)), dma((2 * steps,)),
-            dma((2 * steps,)), dma((2 * steps,)),
+            dma((tiles,)), dma((tiles,)),
+            dma((2 * tiles,)), dma((2 * tiles,)),
+            dma((2 * tiles,)), dma((2 * tiles,)),
+            dma((tiles,)), dma((tiles,)),
         ],
         compiler_params=pltpu.CompilerParams(
             collective_id=0, has_side_effects=True, vmem_limit_bytes=VMEM_LIMIT
@@ -365,7 +398,18 @@
         tokens[0], norm_gain, expert_ids[0].T, gate_values[0].T,
         gate_weight[0], up_weight[0], down_weight[0],
     )
-    return handed[None]
+    copied = pl.pallas_call(
+        copy_out,
+        out_shape=jax.ShapeDtypeStruct((count, model), BF16),
+        in_specs=[hbm],
+        out_specs=hbm,
+        scratch_shapes=[dma((COPIES,))],
+        compiler_params=pltpu.CompilerParams(vmem_limit_bytes=VMEM_LIMIT),
+        cost_estimate=pl.CostEstimate(
+            flops=0, bytes_accessed=4 * count * model, transcendentals=0
+        ),
+    )(handed)
+    return copied[None]
 
 
 VMEM_LIMIT = 63 * 1024 * 1024

time: 71.7 us -> 104 us (1.45)
  Pallas kernels: 69.3 us -> 104 us
  local copies, waits for them, and re-layouts: 2.16 us -> 0 us
    pallas_call x0 -> x1, Pallas kernels: none -> 29 us  [two_chips(): pl.pallas_call(copy_out, out_shape=jax.ShapeDtypeStruct((count, model), B...]
    pallas_call x1, Pallas kernels: 69.3 us -> 75 us  [two_chips(): pl.pallas_call(functools.partial(kernel, sections), out_shape=jax.ShapeDt...]
    unnamed x1 -> x0, local copies, waits for them, and re-layouts: 2.16 us -> none
where the time goes in v2:
time: 104 us
  Pallas kernels  104 us (100%)
    pallas_call x1, Pallas kernels, two_chips(): pl.pallas_call(functools.partial(kernel, sections), out_shape=jax.ShapeDt...  75 us
    pallas_call x1, Pallas kernels, two_chips(): pl.pallas_call(copy_out, out_shape=jax.ShapeDtypeStruct((count, model), B...  29 us

profile of v2, /device:TPU:1, one launch (start us, length us, event | category | flops | bytes accessed | tf_op | source)
XLA Modules:
  0.0 104.0 jit_solution(5553296466717220314)
XLA Ops:
  0.0 75.0 %shard_map.73.src = bf16[128,3584]{1,0:T(8,128)(2,1)} custom-call(bf16[128,3584]{1,0:T(8,128)(2,1)} %bitcast.14, f32[1,3584]{1,0:T(1,128)} %gain.1, s32[2,128]{1,0:T(2,128)} %bitcast.15, f32[2,128]{1,0:T(2,128)} %bitcast.16, bf16[3584,2048]{1,0:T(8,128)(2,1)} %bitcast.11, bf16[3584,2048]{1,0:T(8,128)(2,1)} %bitcast.12, bf16[2048,3584]{1,0:T(8,128)(2,1)} %bitcast.13), custom_call_target="tpu_custom_call" | custom-call | flops 14092861440 | bytes 44040192 | tf_op jit(solution)/shard_map/pallas_call | solution.py:359
  75.0 29.0 %shard_map.74 = bf16[128,3584]{1,0:T(8,128)(2,1)} custom-call(bf16[128,3584]{1,0:T(8,128)(2,1)} %shard_map.73.src), custom_call_target="tpu_custom_call" | custom-call | bytes 1835008 | tf_op jit(solution)/shard_map/pallas_call | solution.py:401

commit v3 on v2

--- a/solution.py
+++ b/solution.py
@@ -17,12 +17,12 @@
 WIDE = 512
 NARROW = 256
 STEP = 16
-COPIES = 8
+COPIES = 4
 
 
 def kernel(
     sections, tok, gain, ids, gates, gate_hbm, up_hbm, down_hbm, out,
-    gate_w, up_w, down_w, nrm, meta, pick, scale, rows_in, hidden, base, local_out, local_in,
+    gate_w, up_w, down_w, nrm, meta, pick, put, scale, rows_in, hidden, base, local_out, local_in,
     far_out, far_in, back,
     w_sem, meta_s, meta_r, sib_s, sib_r, x_s, x_r, relay_s, relay_r, local_s, local_r,
     swap_s, swap_r, back_s, back_r, hand_s, hand_r,
@@ -71,11 +71,9 @@
             down_hbm.at[:, cols], down_w.at[:, cols], w_sem.at[2 * UP_CHUNKS + k]
         )
 
-    for k in range(UP_CHUNKS):
+    for k in range(2):
         gate_copy(k).start()
         up_copy(k).start()
-    for k in range(model // WIDE):
-        down_copy(k).start()
 
     meta[0] = jnp.zeros(meta.shape[1:], F32)
     meta[0, 0:TOP, :] = ids[...].astype(F32)
@@ -131,6 +129,8 @@
         x_copy(0).start()
 
     x_copy(1).start()
+    gate_copy(2).start()
+    up_copy(2).start()
 
     def meta_arrived(slot):
         remote(
@@ -156,6 +156,7 @@
         wanted = lax.broadcasted_iota(jnp.int32, (CAP, tokens), 0).astype(F32)
         picked = jnp.where(ahead == wanted, 1.0, 0.0) * chosen
         pick[place] = picked.astype(BF16)
+        put[place] = picked.T.astype(BF16)
         scale[place] = jnp.broadcast_to(
             jnp.sum(picked * weight, axis=1, keepdims=True), (CAP, scale.shape[2])
         )
@@ -177,9 +178,7 @@
         weighted = (
             product[place * CAP:(place + 1) * CAP, :] * scale[place][:, 0:1]
         ).astype(BF16)
-        return lax.dot_general(
-            pick[place], weighted, (((0,), (0,)), ((), ())), preferred_element_type=F32
-        )
+        return jnp.dot(put[place], weighted, preferred_element_type=F32)
 
     def wide(n):
         return pl.ds(pl.multiple_of(n * WIDE, WIDE), WIDE)
@@ -231,23 +230,16 @@
             ).astype(BF16)
         hand_copy(n).start()
 
-    def down_pass(source, place, extra):
+    def down_pass(source, extra):
         @pl.loop(0, tiles)
         def _(n):
-            if source == 0:
-                down_copy(n).wait()
             for part in range(WIDE // NARROW):
                 cols = pl.ds(pl.multiple_of(n * WIDE + part * NARROW, NARROW), NARROW)
                 product = jnp.dot(
-                    hidden[0:(place + 1) * CAP, :], down_w[:, cols], preferred_element_type=F32
+                    hidden[0:CAP, :], down_w[:, cols], preferred_element_type=F32
                 )
-                far_out[source, :, cols] = spread(place, product).astype(BF16)
-                if source == 0:
-                    base[:, cols] = tok[:, cols].astype(F32) + spread(0, product)
-                    local_out[:, cols] = spread(1, product).astype(BF16)
+                far_out[source, :, cols] = spread(0, product).astype(BF16)
             swap_copy(source, n).start()
-            if source == 0:
-                local_copy(n).start()
 
             @pl.when(n > 0)
             def _():
@@ -261,20 +253,53 @@
     sib_copy(1, theirs).wait_recv()
     meta_arrived(1)
     gather(1, 1)
-    x_copy(0).wait_recv()
-    relay_copy(0, mine).start()
-    meta_arrived(2)
-    relay_copy(0, theirs).wait_recv()
-    gather(2, 2)
 
     @pl.loop(0, UP_CHUNKS)
     def _(k):
         gate_copy(k).wait()
         up_copy(k).wait()
 
+        @pl.when(k + 3 < UP_CHUNKS)
+        def _():
+            gate_copy(k + 3).start()
+            up_copy(k + 3).start()
+
+        @pl.when(k + 3 >= UP_CHUNKS)
+        def _():
+            down_copy(2 * (k + 3 - UP_CHUNKS)).start()
+            down_copy(2 * (k + 3 - UP_CHUNKS) + 1).start()
+
         @pl.loop(0, up_width // NARROW)
         def _(i):
-            up_tile(3 * CAP, k * (up_width // NARROW) + i)
+            up_tile(2 * CAP, k * (up_width // NARROW) + i)
+
+    @pl.loop(0, tiles)
+    def _(n):
+        down_copy(n).wait()
+
+        @pl.when(n + 6 < tiles)
+        def _():
+            down_copy(n + 6).start()
+
+        for part in range(WIDE // NARROW):
+            cols = pl.ds(pl.multiple_of(n * WIDE + part * NARROW, NARROW), NARROW)
+            product = jnp.dot(hidden[...], down_w[:, cols], preferred_element_type=F32)
+            base[:, cols] = tok[:, cols].astype(F32) + spread(0, product)
+            local_out[:, cols] = spread(1, product).astype(BF16)
+        local_copy(n).start()
+
+        @pl.when(n == 4)
+        def _():
+            x_copy(0).wait_recv()
+            relay_copy(0, mine).start()
+
+    meta_arrived(2)
+    relay_copy(0, theirs).wait_recv()
+    gather(2, 0)
+
+    @pl.loop(0, units // NARROW)
+    def _(i):
+        up_tile(CAP, i)
 
     def relay_next(n):
         @pl.when(n == tiles - 2)
@@ -282,7 +307,7 @@
             x_copy(1).wait_recv()
             relay_copy(1, mine).start()
 
-    down_pass(0, 2, relay_next)
+    down_pass(0, relay_next)
 
     meta_arrived(3)
     relay_copy(1, theirs).wait_recv()
@@ -302,7 +327,7 @@
         def _():
             finish(early + lax.div(n, 2))
 
-    down_pass(1, 0, hand_early)
+    down_pass(1, hand_early)
 
     @pl.when(core == 0)
     def _():
@@ -333,17 +358,19 @@
         copy.wait_send()
 
 
-def copy_out(src, dst, sem):
+def copy_out(src, dst, held, in_sem, out_sem):
     rows = src.shape[0] // COPIES
-    copies = [
-        pltpu.make_async_copy(
-            src.at[pl.ds(k * rows, rows)], dst.at[pl.ds(k * rows, rows)], sem.at[k]
-        )
-        for k in range(COPIES)
-    ]
-    for copy in copies:
+    ins, outs = [], []
+    for k in range(COPIES):
+        part = pl.ds(k * rows, rows)
+        ins.append(pltpu.make_async_copy(src.at[part], held.at[part], in_sem.at[k]))
+        outs.append(pltpu.make_async_copy(held.at[part], dst.at[part], out_sem.at[k]))
+    for copy in ins:
         copy.start()
-    for copy in copies:
+    for k in range(COPIES):
+        ins[k].wait()
+        outs[k].start()
+    for copy in outs:
         copy.wait()
 
 
@@ -352,7 +379,7 @@
     units = gate_weight.shape[2]
     half = count // 2
     tiles = model // WIDE
-    rows = 3 * CAP
+    rows = 2 * CAP
     dma = pltpu.SemaphoreType.DMA
     vmem = pl.BlockSpec(memory_space=pltpu.VMEM)
     hbm = pl.BlockSpec(memory_space=pl.ANY)
@@ -367,8 +394,9 @@
             pltpu.VMEM((units, model), BF16),
             pltpu.VMEM((4, count, model), BF16),
             pltpu.VMEM((4, 8, count), F32),
-            pltpu.VMEM((3, CAP, count), BF16),
-            pltpu.VMEM((3, CAP, 128), F32),
+            pltpu.VMEM((2, CAP, count), BF16),
+            pltpu.VMEM((2, count, CAP), BF16),
+            pltpu.VMEM((2, CAP, 128), F32),
             pltpu.VMEM((rows, model), BF16),
             pltpu.VMEM((rows, units), BF16),
             pltpu.VMEM((count, model), F32),
@@ -403,7 +431,7 @@
         out_shape=jax.ShapeDtypeStruct((count, model), BF16),
         in_specs=[hbm],
         out_specs=hbm,
-        scratch_shapes=[dma((COPIES,))],
+        scratch_shapes=[pltpu.VMEM((count, model), BF16), dma((COPIES,)), dma((COPIES,))],
         compiler_params=pltpu.CompilerParams(vmem_limit_bytes=VMEM_LIMIT),
         cost_estimate=pl.CostEstimate(
             flops=0, bytes_accessed=4 * count * model, transcendentals=0

time: 104 us -> 75 us (0.72)
  Pallas kernels: 104 us -> 74.8 us
    pallas_call x1, Pallas kernels: 29 us -> 2.04 us  [two_chips(): pl.pallas_call(copy_out, out_shape=jax.ShapeDtypeStruct((count, model), B...]
    pallas_call x1, Pallas kernels: 75 us -> 72.8 us  [two_chips(): pl.pallas_call(functools.partial(kernel, sections), out_shape=jax.ShapeDt...]
where the time goes in v3:
time: 75 us; the launch traced here: 74.8 us
  Pallas kernels  74.8 us (100%)
    pallas_call x1, Pallas kernels, two_chips(): pl.pallas_call(functools.partial(kernel, sections), out_shape=jax.ShapeDt...  72.8 us
    pallas_call x1, Pallas kernels, two_chips(): pl.pallas_call(copy_out, out_shape=jax.ShapeDtypeStruct((count, model), B...  2.04 us

profile of v3, /device:TPU:1, one launch (start us, length us, event | category | flops | bytes accessed | tf_op | source)
XLA Modules:
  0.0 74.8 jit_solution(13523994692011587676)
XLA Ops:
  0.0 72.8 %shard_map.73.src = bf16[128,3584]{1,0:T(8,128)(2,1)} custom-call(bf16[128,3584]{1,0:T(8,128)(2,1)} %bitcast.14, f32[1,3584]{1,0:T(1,128)} %gain.1, s32[2,128]{1,0:T(2,128)} %bitcast.15, f32[2,128]{1,0:T(2,128)} %bitcast.16, bf16[3584,2048]{1,0:T(8,128)(2,1)} %bitcast.11, bf16[3584,2048]{1,0:T(8,128)(2,1)} %bitcast.12, bf16[2048,3584]{1,0:T(8,128)(2,1)} %bitcast.13), custom_call_target="tpu_custom_call" | custom-call | flops 14092861440 | bytes 44040192 | tf_op jit(solution)/shard_map/pallas_call | solution.py:386
  72.8 2.0 %shard_map.74 = bf16[128,3584]{1,0:T(8,128)(2,1)} custom-call(bf16[128,3584]{1,0:T(8,128)(2,1)} %shard_map.73.src), custom_call_target="tpu_custom_call" | custom-call | bytes 1835008 | tf_op jit(solution)/shard_map/pallas_call | solution.py:429

commit v4 on v3

--- a/solution.py
+++ b/solution.py
@@ -17,7 +17,6 @@
 WIDE = 512
 NARROW = 256
 STEP = 16
-COPIES = 4
 
 
 def kernel(
@@ -180,37 +179,34 @@
         ).astype(BF16)
         return jnp.dot(put[place], weighted, preferred_element_type=F32)
 
-    def wide(n):
-        return pl.ds(pl.multiple_of(n * WIDE, WIDE), WIDE)
-
     def local_copy(n):
         return remote(
-            local_out.at[:, wide(n)], local_in.at[:, wide(n)], local_s.at[n], local_r.at[n],
+            local_out.at[n], local_in.at[n], local_s.at[n], local_r.at[n],
             expert=sibling,
         )
 
     def swap_copy(source, n):
         return remote(
-            far_out.at[source, theirs, wide(n)], far_in.at[source, :, wide(n)],
+            far_out.at[source, n, theirs], far_in.at[source, n],
             swap_s.at[source * tiles + n], swap_r.at[source * tiles + n], expert=sibling,
         )
 
     def back_copy(source, n):
         return remote(
-            far_out.at[source, mine, wide(n)], back.at[mine, wide(n)],
+            far_out.at[source, n, mine], back.at[n, mine],
             back_s.at[source * tiles + n], back_r.at[core * tiles + n],
             expert=far_chip + source,
         )
 
     def hand_copy(n):
         return remote(
-            back.at[:, wide(n)], out.at[:, wide(n)], hand_s.at[n], hand_r.at[n], section=after
+            back.at[n], out.at[n], hand_s.at[n], hand_r.at[n], section=after
         )
 
     def settle(source, n):
         swap_copy(source, n).wait_recv()
-        far_out[source, mine, wide(n)] = (
-            far_out[source, mine, wide(n)].astype(F32) + far_in[source, :, wide(n)].astype(F32)
+        far_out[source, n, mine, :] = (
+            far_out[source, n, mine, :].astype(F32) + far_in[source, n].astype(F32)
         ).astype(BF16)
         back_copy(source, n).start()
 
@@ -219,14 +215,14 @@
         for sender in range(2):
             rows = pl.ds(sender * half, half)
             remote(
-                back.at[rows, wide(n)], back.at[rows, wide(n)], back_s.at[0],
+                back.at[n, rows], back.at[n, rows], back_s.at[0],
                 back_r.at[sender * tiles + n], expert=far_chip,
             ).wait_recv()
         for first in range(0, tokens, 32):
             rows = pl.ds(first, 32)
-            back[rows, wide(n)] = (
-                base[rows, wide(n)] + local_in[rows, wide(n)].astype(F32)
-                + back[rows, wide(n)].astype(F32)
+            back[n, rows, :] = (
+                base[n, rows, :] + local_in[n, rows, :].astype(F32)
+                + back[n, rows, :].astype(F32)
             ).astype(BF16)
         hand_copy(n).start()
 
@@ -238,7 +234,8 @@
                 product = jnp.dot(
                     hidden[0:CAP, :], down_w[:, cols], preferred_element_type=F32
                 )
-                far_out[source, :, cols] = spread(0, product).astype(BF16)
+                part_cols = pl.ds(part * NARROW, NARROW)
+                far_out[source, n, :, part_cols] = spread(0, product).astype(BF16)
             swap_copy(source, n).start()
 
             @pl.when(n > 0)
@@ -284,8 +281,9 @@
         for part in range(WIDE // NARROW):
             cols = pl.ds(pl.multiple_of(n * WIDE + part * NARROW, NARROW), NARROW)
             product = jnp.dot(hidden[...], down_w[:, cols], preferred_element_type=F32)
-            base[:, cols] = tok[:, cols].astype(F32) + spread(0, product)
-            local_out[:, cols] = spread(1, product).astype(BF16)
+            part_cols = pl.ds(part * NARROW, NARROW)
+            base[n, :, part_cols] = tok[:, cols].astype(F32) + spread(0, product)
+            local_out[n, :, part_cols] = spread(1, product).astype(BF16)
         local_copy(n).start()
 
         @pl.when(n == 4)
@@ -359,17 +357,16 @@
 
 
 def copy_out(src, dst, held, in_sem, out_sem):
-    rows = src.shape[0] // COPIES
     ins, outs = [], []
-    for k in range(COPIES):
-        part = pl.ds(k * rows, rows)
-        ins.append(pltpu.make_async_copy(src.at[part], held.at[part], in_sem.at[k]))
-        outs.append(pltpu.make_async_copy(held.at[part], dst.at[part], out_sem.at[k]))
+    for n in range(src.shape[0]):
+        cols = pl.ds(n * WIDE, WIDE)
+        ins.append(pltpu.make_async_copy(src.at[n], held.at[n], in_sem.at[n]))
+        outs.append(pltpu.make_async_copy(held.at[n], dst.at[:, cols], out_sem.at[n]))
     for copy in ins:
         copy.start()
-    for k in range(COPIES):
-        ins[k].wait()
-        outs[k].start()
+    for n in range(src.shape[0]):
+        ins[n].wait()
+        outs[n].start()
     for copy in outs:
         copy.wait()
 
@@ -385,7 +382,7 @@
     hbm = pl.BlockSpec(memory_space=pl.ANY)
     handed = pl.pallas_call(
         functools.partial(kernel, sections),
-        out_shape=jax.ShapeDtypeStruct((count, model), BF16),
+        out_shape=jax.ShapeDtypeStruct((tiles, count, WIDE), BF16),
         in_specs=[vmem, vmem, vmem, vmem, hbm, hbm, hbm],
         out_specs=hbm,
         scratch_shapes=[
@@ -399,12 +396,12 @@
             pltpu.VMEM((2, CAP, 128), F32),
             pltpu.VMEM((rows, model), BF16),
             pltpu.VMEM((rows, units), BF16),
-            pltpu.VMEM((count, model), F32),
-            pltpu.VMEM((count, model), BF16),
-            pltpu.VMEM((count, model), BF16),
-            pltpu.VMEM((2, count, model), BF16),
-            pltpu.VMEM((2, half, model), BF16),
-            pltpu.VMEM((count, model), BF16),
+            pltpu.VMEM((tiles, count, WIDE), F32),
+            pltpu.VMEM((tiles, count, WIDE), BF16),
+            pltpu.VMEM((tiles, count, WIDE), BF16),
+            pltpu.VMEM((2, tiles, count, WIDE), BF16),
+            pltpu.VMEM((2, tiles, half, WIDE), BF16),
+            pltpu.VMEM((tiles, count, WIDE), BF16),
             dma((2 * UP_CHUNKS + model // WIDE,)),
             dma((3,)), dma((3,)),
             dma((2,)), dma((2,)),
@@ -431,7 +428,7 @@
         out_shape=jax.ShapeDtypeStruct((count, model), BF16),
         in_specs=[hbm],
         out_specs=hbm,
-        scratch_shapes=[pltpu.VMEM((count, model), BF16), dma((COPIES,)), dma((COPIES,))],
+        scratch_shapes=[pltpu.VMEM((tiles, count, WIDE), BF16), dma((tiles,)), dma((tiles,))],
         compiler_params=pltpu.CompilerParams(vmem_limit_bytes=VMEM_LIMIT),
         cost_estimate=pl.CostEstimate(
             flops=0, bytes_accessed=4 * count * model, transcendentals=0

time: 75 us -> 75 us (level)
  no operation moved by 1% of the time
where the time goes in v4:
time: 75 us; the launch traced here: 74.8 us
  Pallas kernels  74.8 us (100%)
    pallas_call x1, Pallas kernels, two_chips(): pl.pallas_call(functools.partial(kernel, sections), out_shape=jax.ShapeDt...  72.8 us
    pallas_call x1, Pallas kernels, two_chips(): pl.pallas_call(copy_out, out_shape=jax.ShapeDtypeStruct((count, model), B...  2.03 us

profile of v4, /device:TPU:1, one launch (start us, length us, event | category | flops | bytes accessed | tf_op | source)
XLA Modules:
  0.0 74.8 jit_solution(2245820121019320763)
XLA Ops:
  0.0 72.8 %shard_map.73.src = bf16[7,128,512]{2,1,0:T(8,128)(2,1)} custom-call(bf16[128,3584]{1,0:T(8,128)(2,1)} %bitcast.14, f32[1,3584]{1,0:T(1,128)} %gain.1, s32[2,128]{1,0:T(2,128)} %bitcast.15, f32[2,128]{1,0:T(2,128)} %bitcast.16, bf16[3584,2048]{1,0:T(8,128)(2,1)} %bitcast.11, bf16[3584,2048]{1,0:T(8,128)(2,1)} %bitcast.12, bf16[2048,3584]{1,0:T(8,128)(2,1)} %bitcast.13), custom_call_target="tpu_custom_call" | custom-call | flops 14092861440 | bytes 44040192 | tf_op jit(solution)/shard_map/pallas_call | solution.py:383
  72.8 2.0 %shard_map.74 = bf16[128,3584]{1,0:T(8,128)(2,1)} custom-call(bf16[7,128,512]{2,1,0:T(8,128)(2,1)} %shard_map.73.src), custom_call_target="tpu_custom_call" | custom-call | bytes 1835008 | tf_op jit(solution)/shard_map/pallas_call | solution.py:426

commit v5 on v4

--- a/solution.py
+++ b/solution.py
@@ -17,6 +17,7 @@
 WIDE = 512
 NARROW = 256
 STEP = 16
+LAG = 3
 
 
 def kernel(
@@ -238,13 +239,15 @@
                 far_out[source, n, :, part_cols] = spread(0, product).astype(BF16)
             swap_copy(source, n).start()
 
-            @pl.when(n > 0)
+            @pl.when(n >= LAG)
             def _():
-                settle(source, n - 1)
+                settle(source, n - LAG)
 
             extra(n)
 
-        settle(source, tiles - 1)
+        @pl.loop(tiles - LAG, tiles)
+        def _(n):
+            settle(source, n)
 
     gather(0, 0)
     sib_copy(1, theirs).wait_recv()

time: 75 us -> 74.8 us (level)
  no operation moved by 1% of the time
where the time goes in v5:
time: 74.8 us; the launch traced here: 74.7 us
  Pallas kernels  74.7 us (100%)
    pallas_call x1, Pallas kernels, two_chips(): pl.pallas_call(functools.partial(kernel, sections), out_shape=jax.ShapeDt...  72.7 us
    pallas_call x1, Pallas kernels, two_chips(): pl.pallas_call(copy_out, out_shape=jax.ShapeDtypeStruct((count, model), B...  2.03 us

profile of v5, /device:TPU:1, one launch (start us, length us, event | category | flops | bytes accessed | tf_op | source)
XLA Modules:
  0.0 74.7 jit_solution(12071778013868007343)
XLA Ops:
  0.0 72.7 %shard_map.73.src = bf16[7,128,512]{2,1,0:T(8,128)(2,1)} custom-call(bf16[128,3584]{1,0:T(8,128)(2,1)} %bitcast.14, f32[1,3584]{1,0:T(1,128)} %gain.1, s32[2,128]{1,0:T(2,128)} %bitcast.15, f32[2,128]{1,0:T(2,128)} %bitcast.16, bf16[3584,2048]{1,0:T(8,128)(2,1)} %bitcast.11, bf16[3584,2048]{1,0:T(8,128)(2,1)} %bitcast.12, bf16[2048,3584]{1,0:T(8,128)(2,1)} %bitcast.13), custom_call_target="tpu_custom_call" | custom-call | flops 14092861440 | bytes 44040192 | tf_op jit(solution)/shard_map/pallas_call | solution.py:386
  72.7 2.0 %shard_map.74 = bf16[128,3584]{1,0:T(8,128)(2,1)} custom-call(bf16[7,128,512]{2,1,0:T(8,128)(2,1)} %shard_map.73.src), custom_call_target="tpu_custom_call" | custom-call | bytes 1835008 | tf_op jit(solution)/shard_map/pallas_call | solution.py:429

commit v6 on v4

--- a/solution.py
+++ b/solution.py
@@ -17,6 +17,7 @@
 WIDE = 512
 NARROW = 256
 STEP = 16
+LAG = 3
 
 
 def kernel(
@@ -127,7 +128,6 @@
     def _():
         x_copy(0).start()
 
-    x_copy(1).start()
     gate_copy(2).start()
     up_copy(2).start()
 
@@ -238,13 +238,11 @@
                 far_out[source, n, :, part_cols] = spread(0, product).astype(BF16)
             swap_copy(source, n).start()
 
-            @pl.when(n > 0)
+            @pl.when((n >= 2) & (n < 2 + 2 * LAG) & (lax.rem(n, 2) == 0))
             def _():
-                settle(source, n - 1)
+                settle(source, lax.div(n, 2) - 1)
 
             extra(n)
-
-        settle(source, tiles - 1)
 
     gather(0, 0)
     sib_copy(1, theirs).wait_recv()
@@ -255,6 +253,11 @@
     def _(k):
         gate_copy(k).wait()
         up_copy(k).wait()
+
+        @pl.when(k == UP_CHUNKS - 1)
+        def _():
+            x_copy(0).wait_send()
+            x_copy(1).start()
 
         @pl.when(k + 3 < UP_CHUNKS)
         def _():
@@ -286,7 +289,7 @@
             local_out[n, :, part_cols] = spread(1, product).astype(BF16)
         local_copy(n).start()
 
-        @pl.when(n == 4)
+        @pl.when(n == 1)
         def _():
             x_copy(0).wait_recv()
             relay_copy(0, mine).start()
@@ -300,7 +303,7 @@
         up_tile(CAP, i)
 
     def relay_next(n):
-        @pl.when(n == tiles - 2)
+        @pl.when(n == 1)
         def _():
             x_copy(1).wait_recv()
             relay_copy(1, mine).start()
@@ -310,32 +313,42 @@
     meta_arrived(3)
     relay_copy(1, theirs).wait_recv()
     gather(3, 0)
-    early = units // NARROW // 2 - 1
-
-    @pl.loop(0, units // NARROW)
+    slots = units // NARROW
+
+    def settle_next(source, n):
+        back_copy(source, n - 2).wait_send()
+        settle(source, n)
+
+    @pl.loop(0, slots)
     def _(i):
         up_tile(CAP, i)
 
-        @pl.when((core == 0) & (i >= 2) & (lax.rem(i, 2) == 0))
-        def _():
-            finish(lax.div(i, 2) - 1)
+        @pl.when(i < tiles - LAG)
+        def _():
+            settle_next(0, i + LAG)
+
+        @pl.when((core == 0) & (i >= 3))
+        def _():
+            finish(i - 3)
 
     def hand_early(n):
-        @pl.when((core == 0) & (n < 5) & (lax.rem(n, 2) == 0))
-        def _():
-            finish(early + lax.div(n, 2))
+        @pl.when((core == 0) & (n < 2 * (tiles - slots + 3)) & (lax.rem(n, 2) == 0))
+        def _():
+            finish(slots - 3 + lax.div(n, 2))
 
     down_pass(1, hand_early)
 
-    @pl.when(core == 0)
-    def _():
-        @pl.loop(early + 3, tiles)
-        def _(n):
-            finish(n)
+    @pl.loop(LAG, tiles)
+    def _(n):
+        settle_next(1, n)
+
+        @pl.when(core == 1)
+        def _():
+            finish(n - LAG)
 
     @pl.when(core == 1)
     def _():
-        @pl.loop(0, tiles)
+        @pl.loop(tiles - LAG, tiles)
         def _(n):
             finish(n)
 
@@ -344,12 +357,15 @@
         hand_copy(n).wait()
         local_copy(n).wait_send()
         for source in range(2):
-            back_copy(source, n).wait_send()
             swap_copy(source, n).wait_send()
 
+            @pl.when((n < LAG - 2) | (n >= tiles - 2))
+            def _():
+                back_copy(source, n).wait_send()
+
     for source in range(2):
-        x_copy(source).wait_send()
         relay_copy(source, mine).wait_send()
+    x_copy(1).wait_send()
     sib_copy(0, theirs).wait_send()
     sib_copy(1, mine).wait_send()
     for copy in meta_copies:

time: 75 us -> 74.1 us (0.988)
  Pallas kernels: 74.8 us -> 73.9 us
    pallas_call x1, Pallas kernels: 72.8 us -> 71.9 us  [two_chips(): pl.pallas_call(functools.partial(kernel, sections), out_shape=jax.ShapeDt...]
where the time goes in v6:
time: 74.1 us; the launch traced here: 73.9 us
  Pallas kernels  73.9 us (100%)
    pallas_call x1, Pallas kernels, two_chips(): pl.pallas_call(functools.partial(kernel, sections), out_shape=jax.ShapeDt...  71.9 us
    pallas_call x1, Pallas kernels, two_chips(): pl.pallas_call(copy_out, out_shape=jax.ShapeDtypeStruct((count, model), B...  2.03 us

profile of v6, /device:TPU:1, one launch (start us, length us, event | category | flops | bytes accessed | tf_op | source)
XLA Modules:
  0.0 73.9 jit_solution(1846377424292135674)
XLA Ops:
  0.0 71.9 %shard_map.73.src = bf16[7,128,512]{2,1,0:T(8,128)(2,1)} custom-call(bf16[128,3584]{1,0:T(8,128)(2,1)} %bitcast.14, f32[1,3584]{1,0:T(1,128)} %gain.1, s32[2,128]{1,0:T(2,128)} %bitcast.15, f32[2,128]{1,0:T(2,128)} %bitcast.16, bf16[3584,2048]{1,0:T(8,128)(2,1)} %bitcast.11, bf16[3584,2048]{1,0:T(8,128)(2,1)} %bitcast.12, bf16[2048,3584]{1,0:T(8,128)(2,1)} %bitcast.13), custom_call_target="tpu_custom_call" | custom-call | flops 14092861440 | bytes 44040192 | tf_op jit(solution)/shard_map/pallas_call | solution.py:399
  71.9 2.0 %shard_map.74 = bf16[128,3584]{1,0:T(8,128)(2,1)} custom-call(bf16[7,128,512]{2,1,0:T(8,128)(2,1)} %shard_map.73.src), custom_call_target="tpu_custom_call" | custom-call | bytes 1835008 | tf_op jit(solution)/shard_map/pallas_call | solution.py:442

commit v7 on v6

--- a/solution.py
+++ b/solution.py
@@ -15,7 +15,7 @@
 BF16 = jnp.bfloat16
 UP_CHUNKS = 4
 WIDE = 512
-NARROW = 256
+NARROW = 512
 STEP = 16
 LAG = 3
 
@@ -327,14 +327,14 @@
         def _():
             settle_next(0, i + LAG)
 
-        @pl.when((core == 0) & (i >= 3))
-        def _():
-            finish(i - 3)
+        @pl.when((core == 0) & (i >= 2))
+        def _():
+            finish(i - 2)
 
     def hand_early(n):
-        @pl.when((core == 0) & (n < 2 * (tiles - slots + 3)) & (lax.rem(n, 2) == 0))
-        def _():
-            finish(slots - 3 + lax.div(n, 2))
+        @pl.when((core == 0) & (n < tiles - slots + 2))
+        def _():
+            finish(slots - 2 + n)
 
     down_pass(1, hand_early)
 

time: 74.1 us -> 66.8 us (0.901)
  Pallas kernels: 73.9 us -> 66.7 us
    pallas_call x1, Pallas kernels: 71.9 us -> 64.6 us  [two_chips(): pl.pallas_call(functools.partial(kernel, sections), out_shape=jax.ShapeDt...]
where the time goes in v7:
time: 66.8 us; the launch traced here: 66.7 us
  Pallas kernels  66.7 us (100%)
    pallas_call x1, Pallas kernels, two_chips(): pl.pallas_call(functools.partial(kernel, sections), out_shape=jax.ShapeDt...  64.6 us
    pallas_call x1, Pallas kernels, two_chips(): pl.pallas_call(copy_out, out_shape=jax.ShapeDtypeStruct((count, model), B...  2.03 us

profile of v7, /device:TPU:1, one launch (start us, length us, event | category | flops | bytes accessed | tf_op | source)
XLA Modules:
  0.0 66.7 jit_solution(1429995184018452921)
XLA Ops:
  0.0 64.6 %shard_map.73.src = bf16[7,128,512]{2,1,0:T(8,128)(2,1)} custom-call(bf16[128,3584]{1,0:T(8,128)(2,1)} %bitcast.14, f32[1,3584]{1,0:T(1,128)} %gain.1, s32[2,128]{1,0:T(2,128)} %bitcast.15, f32[2,128]{1,0:T(2,128)} %bitcast.16, bf16[3584,2048]{1,0:T(8,128)(2,1)} %bitcast.11, bf16[3584,2048]{1,0:T(8,128)(2,1)} %bitcast.12, bf16[2048,3584]{1,0:T(8,128)(2,1)} %bitcast.13), custom_call_target="tpu_custom_call" | custom-call | flops 14092861440 | bytes 44040192 | tf_op jit(solution)/shard_map/pallas_call | solution.py:399
  64.6 2.0 %shard_map.74 = bf16[128,3584]{1,0:T(8,128)(2,1)} custom-call(bf16[7,128,512]{2,1,0:T(8,128)(2,1)} %shard_map.73.src), custom_call_target="tpu_custom_call" | custom-call | bytes 1835008 | tf_op jit(solution)/shard_map/pallas_call | solution.py:442
